TPU v7x, 32 devices: a whole 2x2x4 slice. The times are simulated.
32 devices in a mesh: tm: 8 (over z, core), space: 4 (over y, x).
Axes of the slice: x: 2, y: 2, z: 4, core: 2. Of those that a mesh axis runs over, the one named last changes fastest.
Arguments:
- queries: bfloat16 [8, 512, 48, 128], P('tm', 'space'), may hold values from -14 to 14
- noisy_keys: bfloat16 [8, 512, 48, 128], P('tm', 'space'), may hold values from -14 to 14
- noisy_values: bfloat16 [8, 512, 48, 128], P('tm', 'space'), may hold values from -6 to 6
- cache_keys: bfloat16 [8, 512, 48, 128], P('tm', 'space'), may hold values from -12 to 12
- cache_values: bfloat16 [8, 512, 48, 128], P('tm', 'space'), may hold values from -6 to 6
- block_list: int32 [8, 4, 12], P('tm'), may hold values from 0 to 15, as said below
- block_count: int32 [8, 4], P('tm'), may hold values from 1 to 12
- valid_tokens: int32 [8], replicated, may hold values from 385 to 512
Outputs:
- attended: bfloat16 [8, 512, 48, 128], P('tm', 'space')
Inputs may be any that keep to these rules, and one draw needn't show every extreme that they name: `block_list`: entries index the 16 key blocks of stretch c's window in order of offset, the last 4 being stretch c's own blocks. The first block_count[c, a] entries are distinct and name only blocks of stretches 0 or later; the first of them is query block a's own block; later entries repeat that own block.
All inputs are finite; a program needn't handle non-finite values.
Results may differ from a plain program's by a relative error of at most 0.0035.
Values may be sent and summed in bfloat16 or wider, within the bound.
A program may use at most 128 MiB of HBM per device.

v0:
```python
import math

import jax
import jax.numpy as jnp
from jax import lax
from jax.sharding import PartitionSpec as P

BLOCK = 128
WIN = 4
LIST = 12


NEG = -1e30


def passed_along(block, axis, distance):
    devices = range(lax.axis_size(axis))
    route = [(i - distance, i) for i in devices if i - distance in devices]
    return lax.ppermute(block, axis, route)


def hand_forward(pair):
    earlier = []
    carried = pair
    for distance in range(1, WIN):
        carried = passed_along(carried, "tm", 1)
        earlier.append(carried)
    return earlier


def on_device(
    queries,
    noisy_keys,
    noisy_values,
    cache_keys,
    cache_values,
    block_list,
    block_count,
    valid_tokens,
):
    stretch_now = lax.axis_index("tm")
    fresh = jnp.concatenate((queries, noisy_keys, noisy_values), 0)
    fresh = lax.all_to_all(fresh, "space", split_axis=2, concat_axis=1, tiled=True)
    own_cache = jnp.concatenate((cache_keys, cache_values), 0)
    mine = lax.all_to_all(own_cache, "space", split_axis=2, concat_axis=1, tiled=True)
    earlier = hand_forward(mine)
    past = jnp.stack(earlier[::-1], 0)
    stretch_len = fresh.shape[1]
    local_heads = fresh.shape[2]
    head_size = fresh.shape[3]
    block_total = stretch_len // BLOCK
    fresh_heads = jnp.transpose(fresh, (0, 2, 1, 3))
    past_heads = jnp.transpose(past, (1, 3, 0, 2, 4))
    window_keys = jnp.concatenate((past_heads[0], fresh_heads[1][:, None]), 1)
    window_values = jnp.concatenate((past_heads[1], fresh_heads[2][:, None]), 1)
    query_blocks = fresh_heads[0].reshape(local_heads, block_total, BLOCK, head_size)
    key_blocks = window_keys.reshape(local_heads, WIN * block_total, BLOCK, head_size)
    value_blocks = window_values.reshape(local_heads, WIN * block_total, BLOCK, head_size)
    positions = jnp.arange(stretch_len)
    sources = stretch_now - (WIN - 1) + jnp.arange(WIN)
    lengths = valid_tokens[jnp.clip(sources, 0, valid_tokens.shape[0] - 1)]
    key_live = ((sources[:, None] >= 0) & (positions[None, :] < lengths[:, None])).reshape(
        WIN * block_total, BLOCK
    )
    stretch_lists = block_list[0]
    stretch_counts = block_count[0]
    score_scale = 1.0 / math.sqrt(head_size)
    start_best = jnp.full((local_heads, block_total, BLOCK), NEG, jnp.float32)
    start_total = jnp.zeros((local_heads, block_total, BLOCK), jnp.float32)
    start_accum = jnp.zeros((local_heads, block_total, BLOCK, head_size), jnp.float32)

    def slot_step(slot_index, carry):
        row_best, row_total, accum = carry
        chosen = lax.dynamic_slice_in_dim(stretch_lists, slot_index, 1, 1)[:, 0]
        keys_here = key_blocks[:, chosen]
        values_here = value_blocks[:, chosen]
        scores = (
            jnp.einsum(
                "haqd,hakd->haqk", query_blocks, keys_here, preferred_element_type=jnp.float32
            )
            * score_scale
        )
        allowed = (slot_index < stretch_counts)[None, :, None, None] & key_live[chosen][
            None, :, None, :
        ]
        scores = jnp.where(allowed, scores, NEG)
        new_best = jnp.maximum(row_best, jnp.max(scores, axis=-1))
        weights = jnp.where(allowed, jnp.exp(scores - new_best[..., None]), 0.0)
        shrink = jnp.exp(row_best - new_best)
        row_total = row_total * shrink + jnp.sum(weights, axis=-1)
        pieces = jnp.einsum(
            "haqk,hakd->haqd",
            weights.astype(jnp.bfloat16),
            values_here,
            preferred_element_type=jnp.float32,
        )
        accum = accum * shrink[..., None] + pieces
        return (new_best, row_total, accum)

    row_best, row_total, accum = lax.fori_loop(
        0, LIST, slot_step, (start_best, start_total, start_accum)
    )
    mixed_rows = accum / row_total[..., None]
    mixed_rows = mixed_rows.reshape(local_heads, stretch_len, head_size)
    query_live = positions < valid_tokens[stretch_now]
    masked = jnp.where(query_live[None, :, None], mixed_rows, 0.0).astype(jnp.bfloat16)
    attended_local = jnp.transpose(masked, (1, 0, 2))
    return lax.all_to_all(attended_local[None], "space", split_axis=1, concat_axis=2, tiled=True)


def solution(mesh):
    placed = (
        P("tm", "space", None, None),
        P("tm", "space", None, None),
        P("tm", "space", None, None),
        P("tm", "space", None, None),
        P("tm", "space", None, None),
        P("tm", None, None),
        P("tm", None),
        P(),
    )
    return jax.shard_map(
        on_device,
        mesh=mesh,
        in_specs=placed,
        out_specs=P("tm", "space", None, None),
        check_vma=False,
    )
```

profile of v0, /device:TPU:16, one launch (start us, length us, event | category | flops | bytes accessed | tf_op | source)
XLA Modules:
  0.0 447.3 jit_solution(2452081712950554829)
XLA Ops:
  2.7 40.1 %all_to_all.54 = bf16[2,128,48,128]{3,1,0,2:T(8,128)(2,1)S(1)} all-to-all(bf16[2,128,48,128]{3,1,0,2:T(8,128)(2,1)S(1)} %pad_maximum_fusion.3), channel_id=1, replica_groups=mesh['tm'=8,'space'=4] {'space'}, dimensions={2} | all-to-all | bytes 6291456 | tf_op jit(solution)/shard_map/all_to_all | solution.py:45
  45.4 36.7 %collective-permute-done = bf16[2,512,12,128]{3,1,2,0:T(8,128)(2,1)S(1)} collective-permute-done((bf16[2,512,12,128]{3,1,2,0:T(8,128)(2,1)S(1)}, bf16[2,512,12,128]{3,1,2,0:T(8,128)(2,1)S(1)}, u32[]{:S(2)}, u32[]{:S(2)}) %collective-permute-start) | collective-permute-done | bytes 3145760 | tf_op jit(solution)/shard_map/ppermute | solution.py:19
  87.7 5.1 %all-to-all-start.1 = ((bf16[3,128,48,128]{3,1,0,2:T(8,128)(2,1)}), bf16[3,128,48,128]{3,1,0,2:T(8,128)(2,1)}, u32[]{:S(2)}, u32[]{:S(2)}) async-start(bf16[3,128,48,128]{3,1,0,2:T(8,128)(2,1)} %pad_maximum_fusion.2), calls=%async_computation.1 | async-start | bytes 9437184 | tf_op jit(solution)/shard_map/all_to_all | solution.py:43
  92.8 28.0 %collective-permute-done.1 = bf16[2,512,12,128]{3,1,2,0:T(8,128)(2,1)} collective-permute-done((bf16[2,512,12,128]{3,1,2,0:T(8,128)(2,1)S(1)}, bf16[2,512,12,128]{3,1,2,0:T(8,128)(2,1)}, u32[]{:S(2)}, u32[]{:S(2)}) %collective-permute-start.1) | collective-permute-done | bytes 3145760 | tf_op jit(solution)/shard_map/ppermute | solution.py:19
  125.3 21.2 %all-to-all-done.1 = bf16[3,128,48,128]{3,1,0,2:T(8,128)(2,1)} async-done(((bf16[3,128,48,128]{3,1,0,2:T(8,128)(2,1)}), bf16[3,128,48,128]{3,1,0,2:T(8,128)(2,1)}, u32[]{:S(2)}, u32[]{:S(2)}) %all-to-all-start.1) | async-done | bytes 4718624 | tf_op jit(solution)/shard_map/all_to_all | solution.py:43
  152.3 7.2 %collective-permute-done.2 = bf16[2,512,12,128]{3,1,2,0:T(8,128)(2,1)S(1)} collective-permute-done((bf16[2,512,12,128]{3,1,2,0:T(8,128)(2,1)}, bf16[2,512,12,128]{3,1,2,0:T(8,128)(2,1)S(1)}, u32[]{:S(2)}, u32[]{:S(2)}) %collective-permute-start.2) | collective-permute-done | bytes 3145760 | tf_op jit(solution)/shard_map/ppermute | solution.py:19
  161.2 4.8 %maximum_bitcast_fusion = bf16[2,12,3,512,128]{4,3,1,0,2:T(8,128)(2,1)S(1)} fusion(bf16[1,2,512,12,128]{4,2,3,1,0:T(8,128)(2,1)S(1)} %bitcast.89, bf16[1,2,512,12,128]{4,2,3,1,0:T(8,128)(2,1)} %bitcast.8, bf16[1,2,512,12,128]{4,2,3,1,0:T(8,128)(2,1)} %bitcast.90), kind=kLoop, calls=%fused_computation.36 | loop fusion | flops 9437184 | bytes 18874368 | tf_op jit(solution)/shard_map/transpose | solution.py:53
  170.6 5.4 %pad_maximum_fusion = (bf16[12,4,512,128]{3,2,0,1:T(8,128)(2,1)S(1)}, bf16[12,4,512,128]{3,2,0,1:T(8,128)(2,1)S(1)}) fusion(bf16[12,1,512,128]{3,2,0,1:T(8,128)(2,1)} %get-tuple-element.313, bf16[12,3,512,128]{3,2,0,1:T(8,128)(2,1)} %get-tuple-element.310, bf16[12,1,512,128]{3,2,0,1:T(8,128)(2,1)} %get-tuple-element.311, ...), kind=kLoop, calls=%fused_computation.37 | loop fusion | flops 6291456 | bytes 25165824 | tf_op jit(solution)/shard_map/concatenate | solution.py:54
  182.1 229.6 %while.18 = (s32[]{:T(128)}, f32[12,4,128]{2,1,0:T(4,128)S(1)}, f32[12,4,128]{2,1,0:T(4,128)S(1)}, f32[12,4,128,128]{3,2,1,0:T(8,128)}, s32[4]{0:T(128)S(1)}, /*...) while((s32[]{:T(128)}, f32[12,4,128]{2,1,0:T(4,128)S(1)}, ...), condition=%wide.region_3.4_spmd.clone, body=%wide.region_0.3_spmd.clone.sunk | while | flops 415272448 | bytes 27160416 | solution.py:100
  182.9 4.7 %gather_fusion.1 = bf16[4,12,128,128]{3,2,1,0:T(8,128)(2,1)} fusion(bf16[12,16,128,128]{3,2,1,0:T(8,128)(2,1)} %get-tuple-element.431, s32[1024]{0:T(1024)S(1)} %pad_clamp_fusion.3), kind=kCustom, calls=%fused_computation.1.clone.clone.1 | custom fusion | bytes 3145744 | tf_op jit(solution)/shard_map/while/body/eval_jaxpr/gather | solution.py:75
  191.8 4.7 %gather_fusion.2 = bf16[4,12,128,128]{3,2,1,0:T(8,128)(2,1)} fusion(bf16[12,16,128,128]{3,2,1,0:T(8,128)(2,1)} %get-tuple-element.433, s32[1024]{0:T(1024)S(1)} %pad_clamp_fusion.3), kind=kCustom, calls=%fused_computation.2.clone.clone.1 | custom fusion | bytes 3145744 | tf_op jit(solution)/shard_map/while/body/eval_jaxpr/gather | solution.py:76
  201.5 4.7 %gather_fusion.1 = bf16[4,12,128,128]{3,2,1,0:T(8,128)(2,1)} fusion(bf16[12,16,128,128]{3,2,1,0:T(8,128)(2,1)} %get-tuple-element.431, s32[1024]{0:T(1024)S(1)} %pad_clamp_fusion.3), kind=kCustom, calls=%fused_computation.1.clone.clone.1 | custom fusion | bytes 3145744 | tf_op jit(solution)/shard_map/while/body/eval_jaxpr/gather | solution.py:75
  210.4 4.7 %gather_fusion.2 = bf16[4,12,128,128]{3,2,1,0:T(8,128)(2,1)} fusion(bf16[12,16,128,128]{3,2,1,0:T(8,128)(2,1)} %get-tuple-element.433, s32[1024]{0:T(1024)S(1)} %pad_clamp_fusion.3), kind=kCustom, calls=%fused_computation.2.clone.clone.1 | custom fusion | bytes 3145744 | tf_op jit(solution)/shard_map/while/body/eval_jaxpr/gather | solution.py:76
  215.1 4.9 %fusion.44 = f32[12,4,128,128]{3,2,1,0:T(8,128)} fusion(f32[12,4,128,128]{3,2,1,0:T(8,128)} %get-tuple-element.414, f32[12,4,128,128]{3,2,1,0:T(8,128)S(1)} %get-tuple-element.394, f32[12,4,128]{2,1,0:T(4,128)S(1)} %get-tuple-element.396, f32[12,4,128]{2,1,0:T(4,128)S(1)} %select_maximum_fusion.2, pred[]{:T(512)S(6)} %compare.3, ...), kind=kOutput, calls=%fused_computation.10.clone.1 | convolution fusion | flops 207618048 | bytes 11059713 | tf_op jit(solution)/shard_map/while/body/eval_jaxpr/haqk,hakd->haqd/dot_general | solution.py:91
  220.7 4.7 %gather_fusion.1 = bf16[4,12,128,128]{3,2,1,0:T(8,128)(2,1)} fusion(bf16[12,16,128,128]{3,2,1,0:T(8,128)(2,1)} %get-tuple-element.431, s32[1024]{0:T(1024)S(1)} %pad_clamp_fusion.3), kind=kCustom, calls=%fused_computation.1.clone.clone.1 | custom fusion | bytes 3145744 | tf_op jit(solution)/shard_map/while/body/eval_jaxpr/gather | solution.py:75
  229.6 4.7 %gather_fusion.2 = bf16[4,12,128,128]{3,2,1,0:T(8,128)(2,1)} fusion(bf16[12,16,128,128]{3,2,1,0:T(8,128)(2,1)} %get-tuple-element.433, s32[1024]{0:T(1024)S(1)} %pad_clamp_fusion.3), kind=kCustom, calls=%fused_computation.2.clone.clone.1 | custom fusion | bytes 3145744 | tf_op jit(solution)/shard_map/while/body/eval_jaxpr/gather | solution.py:76
  234.3 4.9 %fusion.44 = f32[12,4,128,128]{3,2,1,0:T(8,128)} fusion(f32[12,4,128,128]{3,2,1,0:T(8,128)} %get-tuple-element.414, f32[12,4,128,128]{3,2,1,0:T(8,128)S(1)} %get-tuple-element.394, f32[12,4,128]{2,1,0:T(4,128)S(1)} %get-tuple-element.396, f32[12,4,128]{2,1,0:T(4,128)S(1)} %select_maximum_fusion.2, pred[]{:T(512)S(6)} %compare.3, ...), kind=kOutput, calls=%fused_computation.10.clone.1 | convolution fusion | flops 207618048 | bytes 11059713 | tf_op jit(solution)/shard_map/while/body/eval_jaxpr/haqk,hakd->haqd/dot_general | solution.py:91
  239.9 4.7 %gather_fusion.1 = bf16[4,12,128,128]{3,2,1,0:T(8,128)(2,1)} fusion(bf16[12,16,128,128]{3,2,1,0:T(8,128)(2,1)} %get-tuple-element.431, s32[1024]{0:T(1024)S(1)} %pad_clamp_fusion.3), kind=kCustom, calls=%fused_computation.1.clone.clone.1 | custom fusion | bytes 3145744 | tf_op jit(solution)/shard_map/while/body/eval_jaxpr/gather | solution.py:75
  248.8 4.7 %gather_fusion.2 = bf16[4,12,128,128]{3,2,1,0:T(8,128)(2,1)} fusion(bf16[12,16,128,128]{3,2,1,0:T(8,128)(2,1)} %get-tuple-element.433, s32[1024]{0:T(1024)S(1)} %pad_clamp_fusion.3), kind=kCustom, calls=%fused_computation.2.clone.clone.1 | custom fusion | bytes 3145744 | tf_op jit(solution)/shard_map/while/body/eval_jaxpr/gather | solution.py:76
  253.4 4.9 %fusion.44 = f32[12,4,128,128]{3,2,1,0:T(8,128)} fusion(f32[12,4,128,128]{3,2,1,0:T(8,128)} %get-tuple-element.414, f32[12,4,128,128]{3,2,1,0:T(8,128)S(1)} %get-tuple-element.394, f32[12,4,128]{2,1,0:T(4,128)S(1)} %get-tuple-element.396, f32[12,4,128]{2,1,0:T(4,128)S(1)} %select_maximum_fusion.2, pred[]{:T(512)S(6)} %compare.3, ...), kind=kOutput, calls=%fused_computation.10.clone.1 | convolution fusion | flops 207618048 | bytes 11059713 | tf_op jit(solution)/shard_map/while/body/eval_jaxpr/haqk,hakd->haqd/dot_general | solution.py:91
  259.1 4.7 %gather_fusion.1 = bf16[4,12,128,128]{3,2,1,0:T(8,128)(2,1)} fusion(bf16[12,16,128,128]{3,2,1,0:T(8,128)(2,1)} %get-tuple-element.431, s32[1024]{0:T(1024)S(1)} %pad_clamp_fusion.3), kind=kCustom, calls=%fused_computation.1.clone.clone.1 | custom fusion | bytes 3145744 | tf_op jit(solution)/shard_map/while/body/eval_jaxpr/gather | solution.py:75
  267.9 4.7 %gather_fusion.2 = bf16[4,12,128,128]{3,2,1,0:T(8,128)(2,1)} fusion(bf16[12,16,128,128]{3,2,1,0:T(8,128)(2,1)} %get-tuple-element.433, s32[1024]{0:T(1024)S(1)} %pad_clamp_fusion.3), kind=kCustom, calls=%fused_computation.2.clone.clone.1 | custom fusion | bytes 3145744 | tf_op jit(solution)/shard_map/while/body/eval_jaxpr/gather | solution.py:76
  272.6 4.9 %fusion.44 = f32[12,4,128,128]{3,2,1,0:T(8,128)} fusion(f32[12,4,128,128]{3,2,1,0:T(8,128)} %get-tuple-element.414, f32[12,4,128,128]{3,2,1,0:T(8,128)S(1)} %get-tuple-element.394, f32[12,4,128]{2,1,0:T(4,128)S(1)} %get-tuple-element.396, f32[12,4,128]{2,1,0:T(4,128)S(1)} %select_maximum_fusion.2, pred[]{:T(512)S(6)} %compare.3, ...), kind=kOutput, calls=%fused_computation.10.clone.1 | convolution fusion | flops 207618048 | bytes 11059713 | tf_op jit(solution)/shard_map/while/body/eval_jaxpr/haqk,hakd->haqd/dot_general | solution.py:91
  278.2 4.7 %gather_fusion.1 = bf16[4,12,128,128]{3,2,1,0:T(8,128)(2,1)} fusion(bf16[12,16,128,128]{3,2,1,0:T(8,128)(2,1)} %get-tuple-element.431, s32[1024]{0:T(1024)S(1)} %pad_clamp_fusion.3), kind=kCustom, calls=%fused_computation.1.clone.clone.1 | custom fusion | bytes 3145744 | tf_op jit(solution)/shard_map/while/body/eval_jaxpr/gather | solution.py:75
  291.8 4.9 %fusion.44 = f32[12,4,128,128]{3,2,1,0:T(8,128)} fusion(f32[12,4,128,128]{3,2,1,0:T(8,128)} %get-tuple-element.414, f32[12,4,128,128]{3,2,1,0:T(8,128)S(1)} %get-tuple-element.394, f32[12,4,128]{2,1,0:T(4,128)S(1)} %get-tuple-element.396, f32[12,4,128]{2,1,0:T(4,128)S(1)} %select_maximum_fusion.2, pred[]{:T(512)S(6)} %compare.3, ...), kind=kOutput, calls=%fused_computation.10.clone.1 | convolution fusion | flops 207618048 | bytes 11059713 | tf_op jit(solution)/shard_map/while/body/eval_jaxpr/haqk,hakd->haqd/dot_general | solution.py:91
  311.0 4.9 %fusion.44 = f32[12,4,128,128]{3,2,1,0:T(8,128)} fusion(f32[12,4,128,128]{3,2,1,0:T(8,128)} %get-tuple-element.414, f32[12,4,128,128]{3,2,1,0:T(8,128)S(1)} %get-tuple-element.394, f32[12,4,128]{2,1,0:T(4,128)S(1)} %get-tuple-element.396, f32[12,4,128]{2,1,0:T(4,128)S(1)} %select_maximum_fusion.2, pred[]{:T(512)S(6)} %compare.3, ...), kind=kOutput, calls=%fused_computation.10.clone.1 | convolution fusion | flops 207618048 | bytes 11059713 | tf_op jit(solution)/shard_map/while/body/eval_jaxpr/haqk,hakd->haqd/dot_general | solution.py:91
  330.2 4.9 %fusion.44 = f32[12,4,128,128]{3,2,1,0:T(8,128)} fusion(f32[12,4,128,128]{3,2,1,0:T(8,128)} %get-tuple-element.414, f32[12,4,128,128]{3,2,1,0:T(8,128)S(1)} %get-tuple-element.394, f32[12,4,128]{2,1,0:T(4,128)S(1)} %get-tuple-element.396, f32[12,4,128]{2,1,0:T(4,128)S(1)} %select_maximum_fusion.2, pred[]{:T(512)S(6)} %compare.3, ...), kind=kOutput, calls=%fused_computation.10.clone.1 | convolution fusion | flops 207618048 | bytes 11059713 | tf_op jit(solution)/shard_map/while/body/eval_jaxpr/haqk,hakd->haqd/dot_general | solution.py:91
  349.3 4.9 %fusion.44 = f32[12,4,128,128]{3,2,1,0:T(8,128)} fusion(f32[12,4,128,128]{3,2,1,0:T(8,128)} %get-tuple-element.414, f32[12,4,128,128]{3,2,1,0:T(8,128)S(1)} %get-tuple-element.394, f32[12,4,128]{2,1,0:T(4,128)S(1)} %get-tuple-element.396, f32[12,4,128]{2,1,0:T(4,128)S(1)} %select_maximum_fusion.2, pred[]{:T(512)S(6)} %compare.3, ...), kind=kOutput, calls=%fused_computation.10.clone.1 | convolution fusion | flops 207618048 | bytes 11059713 | tf_op jit(solution)/shard_map/while/body/eval_jaxpr/haqk,hakd->haqd/dot_general | solution.py:91
  368.5 4.9 %fusion.44 = f32[12,4,128,128]{3,2,1,0:T(8,128)} fusion(f32[12,4,128,128]{3,2,1,0:T(8,128)} %get-tuple-element.414, f32[12,4,128,128]{3,2,1,0:T(8,128)S(1)} %get-tuple-element.394, f32[12,4,128]{2,1,0:T(4,128)S(1)} %get-tuple-element.396, f32[12,4,128]{2,1,0:T(4,128)S(1)} %select_maximum_fusion.2, pred[]{:T(512)S(6)} %compare.3, ...), kind=kOutput, calls=%fused_computation.10.clone.1 | convolution fusion | flops 207618048 | bytes 11059713 | tf_op jit(solution)/shard_map/while/body/eval_jaxpr/haqk,hakd->haqd/dot_general | solution.py:91
  387.7 4.9 %fusion.44 = f32[12,4,128,128]{3,2,1,0:T(8,128)} fusion(f32[12,4,128,128]{3,2,1,0:T(8,128)} %get-tuple-element.414, f32[12,4,128,128]{3,2,1,0:T(8,128)S(1)} %get-tuple-element.394, f32[12,4,128]{2,1,0:T(4,128)S(1)} %get-tuple-element.396, f32[12,4,128]{2,1,0:T(4,128)S(1)} %select_maximum_fusion.2, pred[]{:T(512)S(6)} %compare.3, ...), kind=kOutput, calls=%fused_computation.10.clone.1 | convolution fusion | flops 207618048 | bytes 11059713 | tf_op jit(solution)/shard_map/while/body/eval_jaxpr/haqk,hakd->haqd/dot_general | solution.py:91
  406.9 4.9 %fusion.44 = f32[12,4,128,128]{3,2,1,0:T(8,128)} fusion(f32[12,4,128,128]{3,2,1,0:T(8,128)} %get-tuple-element.414, f32[12,4,128,128]{3,2,1,0:T(8,128)S(1)} %get-tuple-element.394, f32[12,4,128]{2,1,0:T(4,128)S(1)} %get-tuple-element.396, f32[12,4,128]{2,1,0:T(4,128)S(1)} %select_maximum_fusion.2, pred[]{:T(512)S(6)} %compare.3, ...), kind=kOutput, calls=%fused_computation.10.clone.1 | convolution fusion | flops 207618048 | bytes 11059713 | tf_op jit(solution)/shard_map/while/body/eval_jaxpr/haqk,hakd->haqd/dot_general | solution.py:91
  417.0 27.6 %all_to_all.55 = bf16[1,512,12,128]{3,2,0,1:T(8,128)(2,1)S(1)} all-to-all(bf16[1,512,12,128]{3,2,0,1:T(8,128)(2,1)S(1)} %bitcast.86), channel_id=1, replica_groups=mesh['tm'=8,'space'=4] {'space'}, dimensions={1} | all-to-all | bytes 3145728 | tf_op jit(solution)/shard_map/all_to_all | solution.py:108
  (215 shorter events, 165.4 us)
Async XLA Ops:
  0.0 1.9 copy-start.4
  42.8 41.2 %copy-start.5 = (bf16[1,128,48,128]{3,2,1,0:T(8,128)(2,1)S(1)}, bf16[1,128,48,128]{3,2,1,0:T(8,128)(2,1)}, u32[]{:S(2)}) copy-start(bf16[1,128,48,128]{3,2,1,0:T(8,128)(2,1)} %param.10) | copy-start | bytes 4718596
  43.2 41.2 %copy-start.6 = (bf16[1,128,48,128]{3,2,1,0:T(8,128)(2,1)S(1)}, bf16[1,128,48,128]{3,2,1,0:T(8,128)(2,1)}, u32[]{:S(2)}) copy-start(bf16[1,128,48,128]{3,2,1,0:T(8,128)(2,1)} %param.11) | copy-start | bytes 4718596
  43.2 41.6 %copy-start.7 = (bf16[1,128,48,128]{3,2,1,0:T(8,128)(2,1)S(1)}, bf16[1,128,48,128]{3,2,1,0:T(8,128)(2,1)}, u32[]{:S(2)}) copy-start(bf16[1,128,48,128]{3,2,1,0:T(8,128)(2,1)} %param.12) | copy-start | bytes 4718596
  43.2 38.9 %collective-permute-start = (bf16[2,512,12,128]{3,1,2,0:T(8,128)(2,1)S(1)}, bf16[2,512,12,128]{3,1,2,0:T(8,128)(2,1)S(1)}, u32[]{:S(2)}, u32[]{:S(2)}) collective-permute-start(bf16[2,512,12,128]{3,1,2,0:T(8,128)(2,1)S(1)} %bitcast.91), channel_id=1, source_target_pairs={{0,4},{4,8},{8,12},{12,16},{16,20},{20,24},{24,28},{1,5},{5,9},{9,... | collective-permute-start | bytes 9437192 | tf_op jit(solution)/shard_map/ppermute | solution.py:19
  82.1 2.8 copy-start.1
  82.1 38.7 %collective-permute-start.1 = (bf16[2,512,12,128]{3,1,2,0:T(8,128)(2,1)S(1)}, bf16[2,512,12,128]{3,1,2,0:T(8,128)(2,1)}, u32[]{:S(2)}, u32[]{:S(2)}) collective-permute-start(bf16[2,512,12,128]{3,1,2,0:T(8,128)(2,1)S(1)} %collective-permute-done), channel_id=1, source_target_pairs={{0,4},{4,8},{8,12},{12,16},{16,20},{20,24},{24,28},{1,5},{5,9},{9,... | collective-permute-start | bytes 9437192 | tf_op jit(solution)/shard_map/ppermute | solution.py:19
  87.7 35.3 %copy-start = (s32[8]{0:T(128)S(1)}, s32[8]{0:T(128)}, u32[]{:S(2)}) copy-start(s32[8]{0:T(128)} %param.17) | copy-start | bytes 100
  87.7 36.2 %copy-start.8 = (s32[1,4,12]{2,1,0:T(4,128)S(1)}, s32[1,4,12]{2,1,0:T(4,128)}, u32[]{:S(2)}) copy-start(s32[1,4,12]{2,1,0:T(4,128)} %param.15) | copy-start | bytes 580
  87.7 58.8 %all-to-all-start.1 = ((bf16[3,128,48,128]{3,1,0,2:T(8,128)(2,1)}), bf16[3,128,48,128]{3,1,0,2:T(8,128)(2,1)}, u32[]{:S(2)}, u32[]{:S(2)}) async-start(bf16[3,128,48,128]{3,1,0,2:T(8,128)(2,1)} %pad_maximum_fusion.2), calls=%async_computation.1 | async-start | bytes 9437184 | tf_op jit(solution)/shard_map/all_to_all | solution.py:43
  120.8 38.8 %collective-permute-start.2 = (bf16[2,512,12,128]{3,1,2,0:T(8,128)(2,1)}, bf16[2,512,12,128]{3,1,2,0:T(8,128)(2,1)S(1)}, u32[]{:S(2)}, u32[]{:S(2)}) collective-permute-start(bf16[2,512,12,128]{3,1,2,0:T(8,128)(2,1)} %collective-permute-done.1), channel_id=1, source_target_pairs={{0,4},{4,8},{8,12},{12,16},{16,20},{20,24},{24,28},{1,5},{5,9},{9,... | collective-permute-start | bytes 9437192 | tf_op jit(solution)/shard_map/ppermute | solution.py:19
  149.8 11.4 %copy-start.2 = (bf16[2,512,12,128]{3,1,2,0:T(8,128)(2,1)S(1)}, bf16[2,512,12,128]{3,1,2,0:T(8,128)(2,1)}, u32[]{:S(2)}) copy-start(bf16[2,512,12,128]{3,1,2,0:T(8,128)(2,1)} %copy-done.1) | copy-start | bytes 9437188
  159.6 1.6 copy-start.3
  179.1 3.0 copy-start.9
where the time goes:
time: 449 us; the launch traced here: 447 us
  local copies, waits for them, and re-layouts  147 us (33%)
  matrix products  95 us (21%)
  waiting for transfers between devices  93.2 us (21%)
  blocking collectives  67.7 us (15%)
  other arithmetic  32.6 us (7%)
  starting transfers between devices  11.3 us (3%)
    ppermute x3, waiting for transfers between devices, passed_along(): return lax.ppermute(block, axis, route)  71.9 us
    dot_general x12, matrix products, slot_step(): jnp.einsum('haqk,hakd->haqd', weights.astype(jnp.bfloat16), values_here,...  57.8 us
    gather x12, local copies, waits for them, and re-layouts, slot_step(): values_here = value_blocks[:, chosen]  56.1 us
    gather x12, local copies, waits for them, and re-layouts, slot_step(): keys_here = key_blocks[:, chosen]  56.1 us
    all_to_all x1, blocking collectives, on_device(): lax.all_to_all(own_cache, 'space', split_axis=2, concat_axis=1, tiled=True)  40.1 us
    dot_general x12, matrix products, slot_step(): jnp.einsum('haqd,hakd->haqk', query_blocks, keys_here, preferred_element_...  37.2 us
    all_to_all x1, blocking collectives, on_device(): lax.all_to_all(attended_local[None], 'space', split_axis=1, concat_axis=2...  27.6 us
    all_to_all x1, waiting for transfers between devices, on_device(): lax.all_to_all(fresh, 'space', split_axis=2, concat_axis=1, tiled=True)  21.2 us
  transfers between devices with their start and end apart: 4, of which 4 were waited for; matrix products, arithmetic and copies ran while one was open for 3% of the time, Pallas kernels for 0%

commit v1 on v0

v1 whole, which is shorter than its diff:
```python
import functools
import math

import jax
import jax.numpy as jnp
from jax import lax
from jax.experimental import pallas as pl
from jax.experimental.pallas import tpu as pltpu
from jax.sharding import PartitionSpec as P

BLOCK = 128
WIN = 4
NEG = -1e30


def window_bias(stretch_now, stretch_len, block_list, block_count, valid_tokens):
    blocks = stretch_len // BLOCK
    slots = jnp.arange(block_list.shape[1])
    used = slots[None, :] < block_count[:, None]
    window_blocks = jnp.arange(WIN * blocks)
    seen = jnp.any(
        (block_list[:, :, None] == window_blocks[None, None, :]) & used[:, :, None], axis=1
    )
    stretches = jnp.arange(valid_tokens.shape[0])
    sources = stretch_now - (WIN - 1) + jnp.arange(WIN)
    lengths = jnp.sum(
        jnp.where(sources[:, None] == stretches[None, :], valid_tokens[None, :], 0), axis=1
    )
    live = (jnp.arange(stretch_len)[None, :] < lengths[:, None]).reshape(-1)
    token_seen = jnp.repeat(seen, BLOCK, axis=1) & live[None, :]
    own = jnp.sum(jnp.where(stretches == stretch_now, valid_tokens, 0))
    row_live = (jnp.arange(stretch_len) < own).astype(jnp.float32)
    bias = jnp.where(token_seen, 0.0, NEG).astype(jnp.float32)
    return bias[:, None, :], row_live[:, None]


def attend(q, k_parts, v_parts, bias, row_live, fold):
    rows = q.shape[0]
    scores = []
    start = 0
    best = None
    for k in k_parts:
        width = k.shape[0]
        s = lax.dot_general(
            q, k, (((1,), (1,)), ((), ())), preferred_element_type=jnp.float32
        )
        s = s.reshape(rows // BLOCK, BLOCK, width) + bias[:, :, start : start + width]
        s = s.reshape(rows, width)
        top = jnp.max(s, axis=1, keepdims=True)
        best = top if best is None else jnp.maximum(best, top)
        scores.append(s)
        start += width
    shift = best * fold
    total = None
    out = None
    for s, v in zip(scores, v_parts):
        w = jnp.exp2(s * fold - shift)
        part = jnp.sum(w, axis=1, keepdims=True)
        o = jnp.dot(w.astype(jnp.bfloat16), v, preferred_element_type=jnp.float32)
        total = part if total is None else total + part
        out = o if out is None else out + o
    return jnp.where(row_live > 0, out / total, 0.0).astype(jnp.bfloat16)


def rows_at_once(stretch_len):
    return BLOCK * max(1, min(stretch_len // BLOCK, (1 << 20) // (WIN * stretch_len * BLOCK)))


def attention_kernel(fold, rows, q_ref, k_ref, v_ref, pk_ref, pv_ref, bias_ref, live_ref, o_ref):
    stretch_len = q_ref.shape[1]
    blocks = rows // BLOCK

    def step(i, carry):
        at = pl.multiple_of(i * rows, rows)
        k_parts = [pk_ref[o, 0] for o in range(WIN - 1)] + [k_ref[0]]
        v_parts = [pv_ref[o, 0] for o in range(WIN - 1)] + [v_ref[0]]
        o_ref[0, pl.ds(at, rows)] = attend(
            q_ref[0, pl.ds(at, rows)],
            k_parts,
            v_parts,
            bias_ref[pl.ds(i * blocks, blocks)],
            live_ref[pl.ds(at, rows)],
            fold,
        )
        return carry

    lax.fori_loop(0, stretch_len // rows, step, 0)


def attention(q, k, v, past_k, past_v, bias, row_live):
    heads, stretch_len, d = q.shape
    fold = math.log2(math.e) / math.sqrt(d)
    rows = rows_at_once(stretch_len)
    one = pl.BlockSpec((1, stretch_len, d), lambda h: (h, 0, 0))
    past = pl.BlockSpec((WIN - 1, 1, stretch_len, d), lambda h: (0, h, 0, 0))
    return pl.pallas_call(
        functools.partial(attention_kernel, fold, rows),
        out_shape=jax.ShapeDtypeStruct(q.shape, q.dtype),
        grid=(heads,),
        in_specs=[
            one,
            one,
            one,
            past,
            past,
            pl.BlockSpec(bias.shape, lambda h: (0, 0, 0)),
            pl.BlockSpec(row_live.shape, lambda h: (0, 0)),
        ],
        out_specs=one,
        compiler_params=pltpu.CompilerParams(vmem_limit_bytes=50 * 1024 * 1024),
        cost_estimate=pl.CostEstimate(
            flops=4 * heads * stretch_len * WIN * stretch_len * d,
            bytes_accessed=2 * (2 + 2 * WIN) * q.size,
            transcendentals=heads * stretch_len * WIN * stretch_len,
        ),
    )(q, k, v, past_k, past_v, bias, row_live)


def on_device(
    queries,
    noisy_keys,
    noisy_values,
    cache_keys,
    cache_values,
    block_list,
    block_count,
    valid_tokens,
):
    stretch_now = lax.axis_index("tm")
    space = lax.axis_size("space")
    stretch_len = queries.shape[1] * space

    def by_heads(*arrays):
        return jnp.transpose(jnp.concatenate(arrays, 0), (0, 2, 1, 3))

    def spread(x):
        return lax.all_to_all(x, "space", split_axis=1, concat_axis=2, tiled=True)

    cache = spread(by_heads(cache_keys, cache_values))
    fresh = spread(by_heads(queries, noisy_keys, noisy_values))
    count = lax.axis_size("tm")
    earlier = []
    carried = cache
    for _ in range(1, WIN):
        carried = lax.ppermute(carried, "tm", [(i, i + 1) for i in range(count - 1)])
        earlier.append(carried)
    past = jnp.stack(earlier[::-1], 0)
    bias, row_live = window_bias(
        stretch_now, stretch_len, block_list[0], block_count[0], valid_tokens
    )
    out = attention(fresh[0], fresh[1], fresh[2], past[:, 0], past[:, 1], bias, row_live)
    back = lax.all_to_all(out, "space", split_axis=1, concat_axis=0, tiled=True)
    return jnp.transpose(back, (1, 0, 2))[None]


def solution(mesh):
    placed = (
        P("tm", "space", None, None),
        P("tm", "space", None, None),
        P("tm", "space", None, None),
        P("tm", "space", None, None),
        P("tm", "space", None, None),
        P("tm", None, None),
        P("tm", None),
        P(),
    )
    return jax.shard_map(
        on_device,
        mesh=mesh,
        in_specs=placed,
        out_specs=P("tm", "space", None, None),
        check_vma=False,
    )
```

time: 449 us -> 241 us (0.54)
  local copies, waits for them, and re-layouts: 147 us -> 23.5 us
  matrix products: 95 us -> 0 us
  Pallas kernels: 0 us -> 33 us
  other arithmetic: 32.6 us -> 12.2 us
    gather x37 -> x0, local copies, waits for them, and re-layouts: 120 us -> none  [the longest x12 56.1 us: slot_step(): values_here = value_blocks[:, chosen]]
    dot_general x24 -> x0, matrix products: 95 us -> none  [the longest x12 57.8 us: slot_step(): jnp.einsum('haqk,hakd->haqd', weights.astype(jnp.bfloat16), values_here,...]
    pallas_call x0 -> x1, Pallas kernels: none -> 33 us  [attention(): pl.pallas_call(functools.partial(attention_kernel, fold, rows), out_shape...]
    reduce_sum x12 -> x2, other arithmetic: 12.3 us -> 0.82 us  [the longest x1 0.64 us: window_bias(): own = jnp.sum(jnp.where(stretches == stretch_now, valid_tokens, 0))]
    concatenate x3 -> x0, other arithmetic: 8.04 us -> none  [the longest x1 5.35 us: on_device(): window_keys = jnp.concatenate((past_heads[0], fresh_heads[1][:, None]), 1)]
    another operation x0 -> x1, other arithmetic: none -> 7.72 us  [on_device(): past = jnp.stack(earlier[::-1], 0)]
    concatenate x2 -> x0, local copies, waits for them, and re-layouts: 6.11 us -> none  [the longest x1 3.08 us: on_device(): window_keys = jnp.concatenate((past_heads[0], fresh_heads[1][:, None]), 1)]
  transfers between devices with their start and end apart: 4 -> 4, of which waited for: 4 -> 4; matrix products, arithmetic and copies ran while one was open for 3% -> 5% of each run, Pallas kernels for 0% -> 0%
where the time goes in v1:
time: 241 us; the launch traced here: 240 us
  waiting for transfers between devices  92.5 us (38%)
  blocking collectives  67.6 us (28%)
  Pallas kernels  33 us (14%)
  local copies, waits for them, and re-layouts  23.5 us (10%)
  other arithmetic  12.2 us (5%)
  starting transfers between devices  11.1 us (5%)
    ppermute x3, waiting for transfers between devices, on_device(): lax.ppermute(carried, 'tm', [(i, i + 1) for i in range(count - 1)])  70.7 us
    all_to_all x1, blocking collectives, spread(): return lax.all_to_all(x, 'space', split_axis=1, concat_axis=2, tiled=True)  40.1 us
    pallas_call x1, Pallas kernels, attention(): pl.pallas_call(functools.partial(attention_kernel, fold, rows), out_shape...  33 us
    all_to_all x1, blocking collectives, on_device(): back = lax.all_to_all(out, 'space', split_axis=1, concat_axis=0, tiled=True)  27.5 us
    all_to_all x1, waiting for transfers between devices, spread(): return lax.all_to_all(x, 'space', split_axis=1, concat_axis=2, tiled=True)  21.9 us
    squeeze x1, local copies, waits for them, and re-layouts, on_device(): past[:, 1]  8.55 us
    another operation x1, other arithmetic, on_device(): past = jnp.stack(earlier[::-1], 0)  7.72 us
    ppermute x3, starting transfers between devices, on_device(): lax.ppermute(carried, 'tm', [(i, i + 1) for i in range(count - 1)])  6 us
  transfers between devices with their start and end apart: 4, of which 4 were waited for; matrix products, arithmetic and copies ran while one was open for 5% of the time, Pallas kernels for 0%

profile of v1, /device:TPU:16, one launch (start us, length us, event | category | flops | bytes accessed | tf_op | source)
XLA Modules:
  0.0 240.2 jit_solution(1360383254874018921)
XLA Ops:
  0.0 1.9 copy.69
  1.9 0.4 copy.70
  2.4 0.3 maximum_bitcast_fusion.1
  2.7 40.1 %all_to_all.51 = bf16[2,48,128,128]{3,2,0,1:T(8,128)(2,1)S(1)} all-to-all(bf16[2,48,128,128]{3,2,0,1:T(8,128)(2,1)S(1)} %maximum_bitcast_fusion.1), channel_id=1, replica_groups=mesh['tm'=8,'space'=4] {'space'}, dimensions={1} | all-to-all | bytes 6291456 | tf_op jit(solution)/shard_map/all_to_all | solution.py:137
  42.8 0.4 copy.72
  43.2 2.2 collective-permute-start
  45.4 36.7 %collective-permute-done = bf16[2,12,512,128]{3,2,1,0:T(8,128)(2,1)S(1)} collective-permute-done((bf16[2,12,512,128]{3,2,1,0:T(8,128)(2,1)S(1)}, bf16[2,12,512,128]{3,2,1,0:T(8,128)(2,1)S(1)}, u32[]{:S(2)}, u32[]{:S(2)}) %collective-permute-start) | collective-permute-done | bytes 3145760 | tf_op jit(solution)/shard_map/ppermute | solution.py:145
  82.1 1.9 collective-permute-start.1
  84.0 0.4 copy.62
  84.4 0.4 copy.63
  84.9 0.4 copy.64
  85.3 2.4 %maximum_bitcast_fusion = bf16[3,48,128,128]{3,2,0,1:T(8,128)(2,1)} fusion(bf16[1,128,48,128]{3,1,0,2:T(8,128)(2,1)S(1)} %copy.64, bf16[1,128,48,128]{3,1,0,2:T(8,128)(2,1)S(1)} %copy.63, bf16[1,128,48,128]{3,1,0,2:T(8,128)(2,1)S(1)} %copy.62), kind=kLoop, calls=%fused_computation.3 | loop fusion | flops 4718592 | bytes 9437184 | tf_op jit(solution)/shard_map/transpose | solution.py:134
  87.7 5.1 %all-to-all-start = ((bf16[3,48,128,128]{3,2,0,1:T(8,128)(2,1)}), bf16[3,48,128,128]{3,2,0,1:T(8,128)(2,1)}, u32[]{:S(2)}, u32[]{:S(2)}) async-start(bf16[3,48,128,128]{3,2,0,1:T(8,128)(2,1)} %maximum_bitcast_fusion), calls=%async_computation | async-start | bytes 9437184 | tf_op jit(solution)/shard_map/all_to_all | solution.py:137
  92.8 28.0 %collective-permute-done.1 = bf16[2,12,512,128]{3,2,1,0:T(8,128)(2,1)} collective-permute-done((bf16[2,12,512,128]{3,2,1,0:T(8,128)(2,1)S(1)}, bf16[2,12,512,128]{3,2,1,0:T(8,128)(2,1)}, u32[]{:S(2)}, u32[]{:S(2)}) %collective-permute-start.1) | collective-permute-done | bytes 3145760 | tf_op jit(solution)/shard_map/ppermute | solution.py:145
  120.8 1.9 collective-permute-start.2
  122.7 0.2 select_reduce_fusion
  123.3 0.6 fusion.4
  124.0 0.7 fusion.live_ref
  124.7 21.9 %all-to-all-done = bf16[3,48,128,128]{3,2,0,1:T(8,128)(2,1)} async-done(((bf16[3,48,128,128]{3,2,0,1:T(8,128)(2,1)}), bf16[3,48,128,128]{3,2,0,1:T(8,128)(2,1)}, u32[]{:S(2)}, u32[]{:S(2)}) %all-to-all-start) | async-done | bytes 4718624 | tf_op jit(solution)/shard_map/all_to_all | solution.py:137
  146.5 3.3 %copy.65 = bf16[3,48,128,128]{3,2,1,0:T(8,128)(2,1)S(1)} copy(bf16[3,48,128,128]{3,2,0,1:T(8,128)(2,1)} %all-to-all-done) | data formatting | bytes 9437184 | tf_op jit(solution)/shard_map/all_to_all | solution.py:137
  149.8 1.0 fusion.5
  150.8 0.2 copy.66
  151.0 1.3 copy.67
  152.3 1.3 copy.68
  153.6 6.0 %collective-permute-done.2 = bf16[2,12,512,128]{3,2,1,0:T(8,128)(2,1)} collective-permute-done((bf16[2,12,512,128]{3,2,1,0:T(8,128)(2,1)}, bf16[2,12,512,128]{3,2,1,0:T(8,128)(2,1)}, u32[]{:S(2)}, u32[]{:S(2)}) %collective-permute-start.2) | collective-permute-done | bytes 3145760 | tf_op jit(solution)/shard_map/ppermute | solution.py:145
  159.7 7.7 %pad_maximum_fusion = bf16[3,2,12,512,128]{4,3,2,0,1:T(8,128)(2,1)} fusion(bf16[1,2,12,512,128]{4,3,2,0,1:T(8,128)(2,1)S(1)} %bitcast.43, bf16[1,2,12,512,128]{4,3,2,0,1:T(8,128)(2,1)} %bitcast.15, bf16[1,2,12,512,128]{4,3,2,0,1:T(8,128)(2,1)} %bitcast.13), kind=kLoop, calls=%fused_computation | loop fusion | flops 9437184 | bytes 18874368 | tf_op jit(solution)/shard_map/stack | solution.py:147
  167.4 8.6 %slice_bitcast_fusion = (bf16[3,12,512,128]{3,2,1,0:T(8,128)(2,1)}, bf16[3,12,512,128]{3,2,1,0:T(8,128)(2,1)}) fusion(bf16[3,2,12,512,128]{4,3,2,0,1:T(8,128)(2,1)} %pad_maximum_fusion), kind=kLoop, calls=%fused_computation.1 | loop fusion | bytes 18874368 | tf_op jit(solution)/shard_map/squeeze | solution.py:151
  175.9 33.0 %shard_map.82 = bf16[12,512,128]{2,1,0:T(8,128)(2,1)S(1)} custom-call(bf16[12,512,128]{2,1,0:T(8,128)(2,1)S(1)} %bitcast.38, bf16[12,512,128]{2,1,0:T(8,128)(2,1)} %bitcast.45, bf16[12,512,128]{2,1,0:T(8,128)(2,1)} %bitcast.46, bf16[3,12,512,128]{3,2,1,0:T(8,128)(2,1)} %get-tuple-element.6.pk_ref, bf16[3,12,512,128]{3,2,1,0:T(8,128)(2,1)} %get-tuple-element.5.pv_ref, ...), custom_call_target="tpu_custom_call" | custom-call | flops 6442450944 | bytes 15728640 | tf_op jit(solution)/shard_map/pallas_call | solution.py:96
  209.0 1.1 copy.77
  210.1 27.5 %all_to_all.52 = bf16[12,512,128]{2,0,1:T(8,128)(2,1)S(1)} all-to-all(bf16[12,512,128]{2,0,1:T(8,128)(2,1)S(1)} %copy.77), channel_id=1, replica_groups=mesh['tm'=8,'space'=4] {'space'}, dimensions={1} | all-to-all | bytes 3145728 | tf_op jit(solution)/shard_map/all_to_all | solution.py:152
  237.6 0.4 copy.79
  238.0 2.2 copy.80
  (23 shorter events, 0.5 us)
Async XLA Ops:
  0.0 1.9 copy-start
  42.8 41.2 %copy-start.1 = (bf16[1,128,48,128]{3,2,1,0:T(8,128)(2,1)S(1)}, bf16[1,128,48,128]{3,2,1,0:T(8,128)(2,1)}, u32[]{:S(2)}) copy-start(bf16[1,128,48,128]{3,2,1,0:T(8,128)(2,1)} %param.8) | copy-start | bytes 4718596
  43.2 41.2 %copy-start.2 = (bf16[1,128,48,128]{3,2,1,0:T(8,128)(2,1)S(1)}, bf16[1,128,48,128]{3,2,1,0:T(8,128)(2,1)}, u32[]{:S(2)}) copy-start(bf16[1,128,48,128]{3,2,1,0:T(8,128)(2,1)} %param.9) | copy-start | bytes 4718596
  43.2 41.6 %copy-start.3 = (bf16[1,128,48,128]{3,2,1,0:T(8,128)(2,1)S(1)}, bf16[1,128,48,128]{3,2,1,0:T(8,128)(2,1)}, u32[]{:S(2)}) copy-start(bf16[1,128,48,128]{3,2,1,0:T(8,128)(2,1)} %param.10) | copy-start | bytes 4718596
  43.2 38.9 %collective-permute-start = (bf16[2,12,512,128]{3,2,1,0:T(8,128)(2,1)S(1)}, bf16[2,12,512,128]{3,2,1,0:T(8,128)(2,1)S(1)}, u32[]{:S(2)}, u32[]{:S(2)}) collective-permute-start(bf16[2,12,512,128]{3,2,1,0:T(8,128)(2,1)S(1)} %bitcast.44), channel_id=1, source_target_pairs={{0,4},{4,8},{8,12},{12,16},{16,20},{20,24},{24,28},{1,5},{5,9},{9,... | collective-permute-start | bytes 9437192 | tf_op jit(solution)/shard_map/ppermute | solution.py:145
  82.1 38.7 %collective-permute-start.1 = (bf16[2,12,512,128]{3,2,1,0:T(8,128)(2,1)S(1)}, bf16[2,12,512,128]{3,2,1,0:T(8,128)(2,1)}, u32[]{:S(2)}, u32[]{:S(2)}) collective-permute-start(bf16[2,12,512,128]{3,2,1,0:T(8,128)(2,1)S(1)} %collective-permute-done), channel_id=1, source_target_pairs={{0,4},{4,8},{8,12},{12,16},{16,20},{20,24},{24,28},{1,5},{5,9},{9,... | collective-permute-start | bytes 9437192 | tf_op jit(solution)/shard_map/ppermute | solution.py:145
  87.7 35.0 %copy-start.6 = (s32[8]{0:T(128)S(1)}, s32[8]{0:T(128)}, u32[]{:S(2)}) copy-start(s32[8]{0:T(128)} %param.15) | copy-start | bytes 100
  87.7 35.3 %copy-start.4 = (s32[1,4,12]{2,1,0:T(4,128)S(1)}, s32[1,4,12]{2,1,0:T(4,128)}, u32[]{:S(2)}) copy-start(s32[1,4,12]{2,1,0:T(4,128)} %param.13) | copy-start | bytes 580
  87.7 35.4 %copy-start.5 = (s32[1,4]{1,0:T(1,128)S(1)}, s32[1,4]{1,0:T(1,128)}, u32[]{:S(2)}) copy-start(s32[1,4]{1,0:T(1,128)} %param.14) | copy-start | bytes 52
  87.7 58.8 %all-to-all-start = ((bf16[3,48,128,128]{3,2,0,1:T(8,128)(2,1)}), bf16[3,48,128,128]{3,2,0,1:T(8,128)(2,1)}, u32[]{:S(2)}, u32[]{:S(2)}) async-start(bf16[3,48,128,128]{3,2,0,1:T(8,128)(2,1)} %maximum_bitcast_fusion), calls=%async_computation | async-start | bytes 9437184 | tf_op jit(solution)/shard_map/all_to_all | solution.py:137
  120.8 38.9 %collective-permute-start.2 = (bf16[2,12,512,128]{3,2,1,0:T(8,128)(2,1)}, bf16[2,12,512,128]{3,2,1,0:T(8,128)(2,1)}, u32[]{:S(2)}, u32[]{:S(2)}) collective-permute-start(bf16[2,12,512,128]{3,2,1,0:T(8,128)(2,1)} %collective-permute-done.1), channel_id=1, source_target_pairs={{0,4},{4,8},{8,12},{12,16},{16,20},{20,24},{24,28},{1,5},{5,9},{9,... | collective-permute-start | bytes 9437192 | tf_op jit(solution)/shard_map/ppermute | solution.py:145

commit v2 on v1

--- a/solution.py
+++ b/solution.py
@@ -11,6 +11,8 @@
 BLOCK = 128
 WIN = 4
 NEG = -1e30
+GROUPS = 6
+MESH = pl.DeviceIdType.MESH
 
 
 def window_bias(stretch_now, stretch_len, block_list, block_count, valid_tokens):
@@ -66,54 +68,281 @@
     return BLOCK * max(1, min(stretch_len // BLOCK, (1 << 20) // (WIN * stretch_len * BLOCK)))
 
 
-def attention_kernel(fold, rows, q_ref, k_ref, v_ref, pk_ref, pv_ref, bias_ref, live_ref, o_ref):
-    stretch_len = q_ref.shape[1]
-    blocks = rows // BLOCK
-
-    def step(i, carry):
-        at = pl.multiple_of(i * rows, rows)
-        k_parts = [pk_ref[o, 0] for o in range(WIN - 1)] + [k_ref[0]]
-        v_parts = [pv_ref[o, 0] for o in range(WIN - 1)] + [v_ref[0]]
-        o_ref[0, pl.ds(at, rows)] = attend(
-            q_ref[0, pl.ds(at, rows)],
-            k_parts,
-            v_parts,
-            bias_ref[pl.ds(i * blocks, blocks)],
-            live_ref[pl.ds(at, rows)],
-            fold,
-        )
+def exchange_kernel(
+    fold,
+    rows,
+    groups,
+    cache_in,
+    fresh_in,
+    bias_ref,
+    live_ref,
+    out,
+    own,
+    past,
+    fresh,
+    mixed,
+    cache_send,
+    cache_recv,
+    fresh_send,
+    fresh_recv,
+    out_send,
+    out_recv,
+    hop_send,
+    hop_recv,
+    here,
+):
+    c, last = lax.axis_index("tm"), lax.axis_size("tm") - 1
+    s, space = lax.axis_index("space"), lax.axis_size("space")
+    tokens = cache_in.shape[2]
+    heads, stretch_len = own.shape[1], own.shape[2]
+    some = heads // groups
+    has_next = c < last
+    hops = WIN - 1
+
+    def part(g):
+        return pl.ds(g * some, some)
+
+    def held_by(p, g):
+        return pl.ds(p * heads + g * some, some)
+
+    def tokens_of(p):
+        return pl.ds(pl.multiple_of(p * tokens, tokens), tokens)
+
+    def spread(src, dst, send, recv, g, apart):
+        p = lax.rem(s + apart, space)
+        return pltpu.make_async_remote_copy(
+            src_ref=src.at[:, held_by(p, g)],
+            dst_ref=dst.at[:, part(g), tokens_of(s)],
+            send_sem=send.at[g, apart - 1],
+            recv_sem=recv.at[g, apart - 1],
+            device_id={"space": p},
+            device_id_type=MESH,
+        )
+
+    def kept(src, dst, kind, g):
+        return pltpu.make_async_copy(
+            src.at[:, held_by(s, g)], dst.at[:, part(g), tokens_of(s)], here.at[kind, g]
+        )
+
+    def cache_copies(g):
+        return [
+            spread(cache_in, own, cache_send, cache_recv, g, apart) for apart in range(1, space)
+        ], kept(cache_in, own, 0, g)
+
+    def fresh_copies(g):
+        return [
+            spread(fresh_in, fresh, fresh_send, fresh_recv, g, apart) for apart in range(1, space)
+        ], kept(fresh_in, fresh, 1, g)
+
+    def out_copies(g):
+        remote = []
+        for apart in range(1, space):
+            p = lax.rem(s + apart, space)
+            remote.append(
+                pltpu.make_async_remote_copy(
+                    src_ref=mixed.at[part(g), tokens_of(p)],
+                    dst_ref=out.at[held_by(s, g)],
+                    send_sem=out_send.at[g, apart - 1],
+                    recv_sem=out_recv.at[g, apart - 1],
+                    device_id={"space": p},
+                    device_id_type=MESH,
+                )
+            )
+        local = pltpu.make_async_copy(
+            mixed.at[part(g), tokens_of(s)], out.at[held_by(s, g)], here.at[2, g]
+        )
+        return remote, local
+
+    def start(copies):
+        remote, local = copies
+        for copy in remote:
+            copy.start()
+        local.start()
+
+    def arrive(copies):
+        remote, local = copies
+        for copy in remote:
+            copy.wait_recv()
+        local.wait()
+
+    def hop(j, g):
+        return pltpu.make_async_remote_copy(
+            src_ref=own.at[:, part(g)] if j == 0 else past.at[j - 1, :, part(g)],
+            dst_ref=past.at[j, :, part(g)],
+            send_sem=hop_send.at[j, g],
+            recv_sem=hop_recv.at[j, g],
+            device_id={"tm": c + 1},
+            device_id_type=MESH,
+        )
+
+    barrier = pltpu.get_barrier_semaphore()
+    for apart in range(1, space):
+        pl.semaphore_signal(
+            barrier,
+            inc=1,
+            device_id={"space": lax.rem(s + apart, space)},
+            device_id_type=MESH,
+        )
+
+    @pl.when(has_next)
+    def _():
+        pl.semaphore_signal(barrier, inc=1, device_id={"tm": c + 1}, device_id_type=MESH)
+
+    @pl.when(c > 0)
+    def _():
+        pl.semaphore_signal(barrier, inc=1, device_id={"tm": c - 1}, device_id_type=MESH)
+
+    pl.semaphore_wait(
+        barrier, space - 1 + jnp.where(has_next, 1, 0) + jnp.where(c > 0, 1, 0)
+    )
+
+    @pl.when(has_next)
+    def _():
+        start(cache_copies(0))
+        if groups > 1:
+            start(cache_copies(1))
+
+    start(fresh_copies(0))
+
+    for j in range(hops):
+
+        @pl.when(c <= j)
+        def _(j=j):
+            def clear(h, carry):
+                for kind in range(2):
+                    past[j, kind, h] = jnp.zeros(past.shape[3:], past.dtype)
+                return carry
+
+            lax.fori_loop(0, heads, clear, 0)
+
+    @pl.when(has_next)
+    def _():
+        arrive(cache_copies(0))
+        hop(0, 0).start()
+
+    def attend_head(h):
+        blocks = rows // BLOCK
+        k_parts = [past.at[hops - 1 - o, 0, h] for o in range(hops)] + [fresh.at[1, h]]
+        v_parts = [past.at[hops - 1 - o, 1, h] for o in range(hops)] + [fresh.at[2, h]]
+
+        def step(i, carry):
+            at = pl.multiple_of(i * rows, rows)
+            mixed[h, pl.ds(at, rows)] = attend(
+                fresh[0, h, pl.ds(at, rows)],
+                [k[...] for k in k_parts],
+                [v[...] for v in v_parts],
+                bias_ref[pl.ds(i * blocks, blocks)],
+                live_ref[pl.ds(at, rows)],
+                fold,
+            )
+            return carry
+
+        lax.fori_loop(0, stretch_len // rows, step, 0)
+
+    def turn(g, carry):
+        @pl.when((g + 2 < groups) & has_next)
+        def _():
+            start(cache_copies(g + 2))
+
+        @pl.when(g + 1 < groups)
+        def _():
+            start(fresh_copies(g + 1))
+
+        for j in range(hops - 1):
+
+            @pl.when((g < groups) & (c >= j + 1))
+            def _(j=j):
+                hop(j, g).wait_recv()
+
+            @pl.when((g < groups) & (c >= j + 1) & has_next)
+            def _(j=j):
+                hop(j + 1, g).start()
+
+        @pl.when((g + 1 < groups) & has_next)
+        def _():
+            arrive(cache_copies(g + 1))
+            hop(0, g + 1).start()
+
+        @pl.when(g > 0)
+        def _():
+            done = g - 1
+
+            @pl.when(c >= hops)
+            def _():
+                hop(hops - 1, done).wait_recv()
+
+            arrive(fresh_copies(done))
+
+            def one(i, carry):
+                attend_head(done * some + i)
+                return carry
+
+            lax.fori_loop(0, some, one, 0)
+            start(out_copies(done))
+
         return carry
 
-    lax.fori_loop(0, stretch_len // rows, step, 0)
-
-
-def attention(q, k, v, past_k, past_v, bias, row_live):
-    heads, stretch_len, d = q.shape
+    lax.fori_loop(0, groups + 1, turn, 0)
+
+    def finish(g, carry):
+        @pl.when(has_next)
+        def _():
+            for copy in cache_copies(g)[0]:
+                copy.wait_send()
+
+        for copy in fresh_copies(g)[0]:
+            copy.wait_send()
+        for j in range(hops):
+
+            @pl.when(has_next & (c >= j))
+            def _(j=j):
+                hop(j, g).wait_send()
+
+        remote, local = out_copies(g)
+        for copy in remote:
+            copy.wait()
+        local.wait()
+        return carry
+
+    lax.fori_loop(0, groups, finish, 0)
+
+
+def exchange_and_attend(cache, fresh, bias, row_live):
+    space = lax.axis_size("space")
+    _, all_heads, tokens, d = fresh.shape
+    heads, stretch_len = all_heads // space, tokens * space
+    groups = max(n for n in range(1, GROUPS + 1) if heads % n == 0)
     fold = math.log2(math.e) / math.sqrt(d)
     rows = rows_at_once(stretch_len)
-    one = pl.BlockSpec((1, stretch_len, d), lambda h: (h, 0, 0))
-    past = pl.BlockSpec((WIN - 1, 1, stretch_len, d), lambda h: (0, h, 0, 0))
+    dma = pltpu.SemaphoreType.DMA
     return pl.pallas_call(
-        functools.partial(attention_kernel, fold, rows),
-        out_shape=jax.ShapeDtypeStruct(q.shape, q.dtype),
-        grid=(heads,),
+        functools.partial(exchange_kernel, fold, rows, groups),
+        out_shape=jax.ShapeDtypeStruct((all_heads, tokens, d), fresh.dtype),
         in_specs=[
-            one,
-            one,
-            one,
-            past,
-            past,
-            pl.BlockSpec(bias.shape, lambda h: (0, 0, 0)),
-            pl.BlockSpec(row_live.shape, lambda h: (0, 0)),
+            pl.BlockSpec(memory_space=pl.ANY),
+            pl.BlockSpec(memory_space=pl.ANY),
+            pl.BlockSpec(memory_space=pltpu.VMEM),
+            pl.BlockSpec(memory_space=pltpu.VMEM),
         ],
-        out_specs=one,
-        compiler_params=pltpu.CompilerParams(vmem_limit_bytes=50 * 1024 * 1024),
+        out_specs=pl.BlockSpec(memory_space=pl.ANY),
+        scratch_shapes=[
+            pltpu.VMEM((2, heads, stretch_len, d), fresh.dtype),
+            pltpu.VMEM((WIN - 1, 2, heads, stretch_len, d), fresh.dtype),
+            pltpu.VMEM((3, heads, stretch_len, d), fresh.dtype),
+            pltpu.VMEM((heads, stretch_len, d), fresh.dtype),
+        ]
+        + [dma((groups, space - 1))] * 6
+        + [dma((WIN - 1, groups))] * 2
+        + [dma((3, groups))],
+        compiler_params=pltpu.CompilerParams(
+            collective_id=0, has_side_effects=True, vmem_limit_bytes=50 * 1024 * 1024
+        ),
         cost_estimate=pl.CostEstimate(
             flops=4 * heads * stretch_len * WIN * stretch_len * d,
-            bytes_accessed=2 * (2 + 2 * WIN) * q.size,
+            bytes_accessed=12 * heads * stretch_len * d,
             transcendentals=heads * stretch_len * WIN * stretch_len,
         ),
-    )(q, k, v, past_k, past_v, bias, row_live)
+    )(cache, fresh, bias, row_live)
 
 
 def on_device(
@@ -133,23 +362,15 @@
     def by_heads(*arrays):
         return jnp.transpose(jnp.concatenate(arrays, 0), (0, 2, 1, 3))
 
-    def spread(x):
-        return lax.all_to_all(x, "space", split_axis=1, concat_axis=2, tiled=True)
-
-    cache = spread(by_heads(cache_keys, cache_values))
-    fresh = spread(by_heads(queries, noisy_keys, noisy_values))
-    count = lax.axis_size("tm")
-    earlier = []
-    carried = cache
-    for _ in range(1, WIN):
-        carried = lax.ppermute(carried, "tm", [(i, i + 1) for i in range(count - 1)])
-        earlier.append(carried)
-    past = jnp.stack(earlier[::-1], 0)
     bias, row_live = window_bias(
         stretch_now, stretch_len, block_list[0], block_count[0], valid_tokens
     )
-    out = attention(fresh[0], fresh[1], fresh[2], past[:, 0], past[:, 1], bias, row_live)
-    back = lax.all_to_all(out, "space", split_axis=1, concat_axis=0, tiled=True)
+    back = exchange_and_attend(
+        by_heads(cache_keys, cache_values),
+        by_heads(queries, noisy_keys, noisy_values),
+        bias,
+        row_live,
+    )
     return jnp.transpose(back, (1, 0, 2))[None]
 
 

time: 241 us -> 140 us (0.58)
  waiting for transfers between devices: 92.5 us -> 0 us
  Pallas kernels: 33 us -> 123 us
  blocking collectives: 67.6 us -> 0 us
  local copies, waits for them, and re-layouts: 23.5 us -> 8.6 us
  starting transfers between devices: 11.1 us -> 0 us
  other arithmetic: 12.2 us -> 8.04 us
    pallas_call x1, Pallas kernels: 33 us -> 123 us  [exchange_and_attend(): pl.pallas_call(functools.partial(exchange_kernel, fold, rows, groups), ou...]
    ppermute x3 -> x0, waiting for transfers between devices: 70.7 us -> none  [on_device(): lax.ppermute(carried, 'tm', [(i, i + 1) for i in range(count - 1)])]
    all_to_all x2 -> x0, blocking collectives: 67.6 us -> none  [the longest x1 40.1 us: spread(): return lax.all_to_all(x, 'space', split_axis=1, concat_axis=2, tiled=True)]
    all_to_all x1 -> x0, waiting for transfers between devices: 21.9 us -> none  [spread(): return lax.all_to_all(x, 'space', split_axis=1, concat_axis=2, tiled=True)]
    squeeze x1 -> x0, local copies, waits for them, and re-layouts: 8.55 us -> none  [on_device(): past[:, 1]]
    another operation x1 -> x0, other arithmetic: 7.72 us -> none  [on_device(): past = jnp.stack(earlier[::-1], 0)]
    ppermute x3 -> x0, starting transfers between devices: 6 us -> none  [on_device(): lax.ppermute(carried, 'tm', [(i, i + 1) for i in range(count - 1)])]
    all_to_all x1 -> x0, starting transfers between devices: 5.07 us -> none  [spread(): return lax.all_to_all(x, 'space', split_axis=1, concat_axis=2, tiled=True)]
  transfers between devices with their start and end apart: 4 -> 0, of which waited for: 4 -> 0; matrix products, arithmetic and copies ran while one was open for 5% -> 0% of each run, Pallas kernels for 0% -> 0%
where the time goes in v2:
time: 140 us
  Pallas kernels  123 us (88%)
  local copies, waits for them, and re-layouts  8.6 us (6%)
  other arithmetic  8.04 us (6%)
    pallas_call x1, Pallas kernels, exchange_and_attend(): pl.pallas_call(functools.partial(exchange_kernel, fold, rows, groups), ou...  123 us
    unnamed x14, local copies, waits for them, and re-layouts  5.57 us
    transpose x2, other arithmetic, by_heads(): return jnp.transpose(jnp.concatenate(arrays, 0), (0, 2, 1, 3))  4.34 us

profile of v2, /device:TPU:16, one launch (start us, length us, event | category | flops | bytes accessed | tf_op | source)
XLA Modules:
  0.0 139.9 jit_solution(5505698397067538305)
XLA Ops:
  0.0 1.3 fusion.4
  1.3 0.8 select_reduce_fusion
  2.1 0.1 fusion.3
  2.2 0.7 iota_compare_fusion.3
  2.9 0.8 copy.27
  3.7 0.1 fusion.2
  3.8 0.1 broadcast_in_dim.40
  3.9 0.7 fusion.live_ref
  4.6 0.0 copy-start
  4.6 1.9 %copy.24 = bf16[1,128,48,128]{3,1,2,0:T(8,128)(2,1)S(1)} copy(bf16[1,128,48,128]{3,2,1,0:T(8,128)(2,1)} %param.8) | data formatting | bytes 3145728 | tf_op args[0]
  6.6 0.0 copy-done
  6.6 0.0 copy-start.1
  6.6 0.4 copy.25
  7.0 1.0 copy-done.1
  8.0 0.4 copy.26
  8.4 0.0 copy-start.2
  8.4 2.4 %maximum_bitcast_fusion.fresh_in = bf16[3,48,128,128]{3,2,1,0:T(8,128)(2,1)} fusion(bf16[1,128,48,128]{3,1,2,0:T(8,128)(2,1)S(1)} %copy.26, bf16[1,128,48,128]{3,1,2,0:T(8,128)(2,1)S(1)} %copy.25, bf16[1,128,48,128]{3,1,2,0:T(8,128)(2,1)S(1)} %copy.24), kind=kLoop, calls=%fused_computation | loop fusion | flops 4718592 | bytes 9437184 | tf_op jit(solution)/shard_map/transpose | solution.py:363
  10.8 0.0 copy-done.2
  10.8 0.0 copy-start.3
  10.8 0.4 copy.22
  11.2 1.0 copy-done.3
  12.2 0.4 copy.23
  12.6 1.9 %maximum_bitcast_fusion.1.cache_in = bf16[2,48,128,128]{3,2,1,0:T(8,128)(2,1)} fusion(bf16[1,128,48,128]{3,1,2,0:T(8,128)(2,1)S(1)} %copy.23, bf16[1,128,48,128]{3,1,2,0:T(8,128)(2,1)S(1)} %copy.22), kind=kLoop, calls=%fused_computation.1 | loop fusion | flops 1572864 | bytes 6291456 | tf_op jit(solution)/shard_map/transpose | solution.py:363
  14.6 123.1 %shard_map.82 = bf16[48,128,128]{2,1,0:T(8,128)(2,1)S(1)} custom-call(bf16[2,48,128,128]{3,2,1,0:T(8,128)(2,1)} %maximum_bitcast_fusion.1.cache_in, bf16[3,48,128,128]{3,2,1,0:T(8,128)(2,1)} %maximum_bitcast_fusion.fresh_in, f32[4,1,2048]{2,1,0:T(1,128)S(1)} %and_select_fusion.bias_ref, f32[512,1]{1,0:T(8,128)S(1)} %fusion.live_ref), custom_call_target="tpu_custom_call" | custom-call | flops 6442450944 | bytes 9437184 | tf_op jit(solution)/shard_map/pallas_call | solution.py:318
  137.7 2.2 %copy.29 = bf16[1,128,48,128]{3,2,1,0:T(8,128)(2,1)} copy(bf16[1,128,48,128]{3,1,2,0:T(8,128)(2,1)S(1)} %bitcast.12) | data formatting | bytes 3145728 | tf_op jit(solution)/shard_map/broadcast_in_dim | solution.py:374
  (4 shorter events, 0.1 us)
Async XLA Ops:
  4.6 1.9 %copy-start = (bf16[1,128,48,128]{3,2,1,0:T(8,128)(2,1)S(1)}, bf16[1,128,48,128]{3,2,1,0:T(8,128)(2,1)}, u32[]{:S(2)}) copy-start(bf16[1,128,48,128]{3,2,1,0:T(8,128)(2,1)} %param.9) | copy-start | bytes 4718596
  6.6 1.4 %copy-start.1 = (bf16[1,128,48,128]{3,2,1,0:T(8,128)(2,1)S(1)}, bf16[1,128,48,128]{3,2,1,0:T(8,128)(2,1)}, u32[]{:S(2)}) copy-start(bf16[1,128,48,128]{3,2,1,0:T(8,128)(2,1)} %param.10) | copy-start | bytes 4718596
  8.4 2.4 %copy-start.2 = (bf16[1,128,48,128]{3,2,1,0:T(8,128)(2,1)S(1)}, bf16[1,128,48,128]{3,2,1,0:T(8,128)(2,1)}, u32[]{:S(2)}) copy-start(bf16[1,128,48,128]{3,2,1,0:T(8,128)(2,1)} %param.11) | copy-start | bytes 4718596
  10.8 1.4 %copy-start.3 = (bf16[1,128,48,128]{3,2,1,0:T(8,128)(2,1)S(1)}, bf16[1,128,48,128]{3,2,1,0:T(8,128)(2,1)}, u32[]{:S(2)}) copy-start(bf16[1,128,48,128]{3,2,1,0:T(8,128)(2,1)} %param.12) | copy-start | bytes 4718596

commit v3 on v2

--- a/solution.py
+++ b/solution.py
@@ -11,29 +11,8 @@
 BLOCK = 128
 WIN = 4
 NEG = -1e30
-GROUPS = 6
+GROUPS = 12
 MESH = pl.DeviceIdType.MESH
-
-
-def window_bias(stretch_now, stretch_len, block_list, block_count, valid_tokens):
-    blocks = stretch_len // BLOCK
-    slots = jnp.arange(block_list.shape[1])
-    used = slots[None, :] < block_count[:, None]
-    window_blocks = jnp.arange(WIN * blocks)
-    seen = jnp.any(
-        (block_list[:, :, None] == window_blocks[None, None, :]) & used[:, :, None], axis=1
-    )
-    stretches = jnp.arange(valid_tokens.shape[0])
-    sources = stretch_now - (WIN - 1) + jnp.arange(WIN)
-    lengths = jnp.sum(
-        jnp.where(sources[:, None] == stretches[None, :], valid_tokens[None, :], 0), axis=1
-    )
-    live = (jnp.arange(stretch_len)[None, :] < lengths[:, None]).reshape(-1)
-    token_seen = jnp.repeat(seen, BLOCK, axis=1) & live[None, :]
-    own = jnp.sum(jnp.where(stretches == stretch_now, valid_tokens, 0))
-    row_live = (jnp.arange(stretch_len) < own).astype(jnp.float32)
-    bias = jnp.where(token_seen, 0.0, NEG).astype(jnp.float32)
-    return bias[:, None, :], row_live[:, None]
 
 
 def attend(q, k_parts, v_parts, bias, row_live, fold):
@@ -61,7 +40,7 @@
         o = jnp.dot(w.astype(jnp.bfloat16), v, preferred_element_type=jnp.float32)
         total = part if total is None else total + part
         out = o if out is None else out + o
-    return jnp.where(row_live > 0, out / total, 0.0).astype(jnp.bfloat16)
+    return jnp.where(row_live, out / total, 0.0).astype(jnp.bfloat16)
 
 
 def rows_at_once(stretch_len):
@@ -72,15 +51,20 @@
     fold,
     rows,
     groups,
-    cache_in,
-    fresh_in,
-    bias_ref,
-    live_ref,
+    ck_in,
+    cv_in,
+    q_in,
+    k_in,
+    v_in,
+    list_ref,
+    count_ref,
+    valid_ref,
     out,
     own,
     past,
     fresh,
     mixed,
+    bias_ref,
     cache_send,
     cache_recv,
     fresh_send,
@@ -89,11 +73,14 @@
     out_recv,
     hop_send,
     hop_recv,
-    here,
+    cache_keep,
+    fresh_keep,
+    out_keep,
 ):
     c, last = lax.axis_index("tm"), lax.axis_size("tm") - 1
     s, space = lax.axis_index("space"), lax.axis_size("space")
-    tokens = cache_in.shape[2]
+    cache_in, fresh_in = (ck_in, cv_in), (q_in, k_in, v_in)
+    tokens = q_in.shape[1]
     heads, stretch_len = own.shape[1], own.shape[2]
     some = heads // groups
     has_next = c < last
@@ -108,31 +95,30 @@
     def tokens_of(p):
         return pl.ds(pl.multiple_of(p * tokens, tokens), tokens)
 
-    def spread(src, dst, send, recv, g, apart):
-        p = lax.rem(s + apart, space)
-        return pltpu.make_async_remote_copy(
-            src_ref=src.at[:, held_by(p, g)],
-            dst_ref=dst.at[:, part(g), tokens_of(s)],
-            send_sem=send.at[g, apart - 1],
-            recv_sem=recv.at[g, apart - 1],
-            device_id={"space": p},
-            device_id_type=MESH,
-        )
-
-    def kept(src, dst, kind, g):
-        return pltpu.make_async_copy(
-            src.at[:, held_by(s, g)], dst.at[:, part(g), tokens_of(s)], here.at[kind, g]
-        )
+    def spread(sources, dst, send, recv, keep, g):
+        remote, local = [], []
+        for kind, src in enumerate(sources):
+            landing = dst.at[kind, part(g), tokens_of(s)]
+            for apart in range(1, space):
+                p = lax.rem(s + apart, space)
+                remote.append(
+                    pltpu.make_async_remote_copy(
+                        src_ref=src.at[held_by(p, g)],
+                        dst_ref=landing,
+                        send_sem=send.at[kind, g, apart - 1],
+                        recv_sem=recv.at[kind, g, apart - 1],
+                        device_id={"space": p},
+                        device_id_type=MESH,
+                    )
+                )
+            local.append(pltpu.make_async_copy(src.at[held_by(s, g)], landing, keep.at[kind, g]))
+        return remote, local
 
     def cache_copies(g):
-        return [
-            spread(cache_in, own, cache_send, cache_recv, g, apart) for apart in range(1, space)
-        ], kept(cache_in, own, 0, g)
+        return spread(cache_in, own, cache_send, cache_recv, cache_keep, g)
 
     def fresh_copies(g):
-        return [
-            spread(fresh_in, fresh, fresh_send, fresh_recv, g, apart) for apart in range(1, space)
-        ], kept(fresh_in, fresh, 1, g)
+        return spread(fresh_in, fresh, fresh_send, fresh_recv, fresh_keep, g)
 
     def out_copies(g):
         remote = []
@@ -149,21 +135,21 @@
                 )
             )
         local = pltpu.make_async_copy(
-            mixed.at[part(g), tokens_of(s)], out.at[held_by(s, g)], here.at[2, g]
+            mixed.at[part(g), tokens_of(s)], out.at[held_by(s, g)], out_keep.at[g]
         )
-        return remote, local
+        return remote, [local]
 
     def start(copies):
         remote, local = copies
-        for copy in remote:
+        for copy in remote + local:
             copy.start()
-        local.start()
 
     def arrive(copies):
         remote, local = copies
         for copy in remote:
             copy.wait_recv()
-        local.wait()
+        for copy in local:
+            copy.wait()
 
     def hop(j, g):
         return pltpu.make_async_remote_copy(
@@ -202,7 +188,21 @@
         if groups > 1:
             start(cache_copies(1))
 
-    start(fresh_copies(0))
+    def see(a, carry):
+        column = lax.broadcasted_iota(jnp.int32, (1, WIN * stretch_len), 1)
+        seen = column < 0
+        for slot in range(list_ref.shape[1]):
+            first = jnp.where(slot < count_ref[a], list_ref[a, slot] * BLOCK, -BLOCK)
+            seen = seen | ((column >= first) & (column < first + BLOCK))
+        live = column < 0
+        for o in range(WIN):
+            source = c - hops + o
+            length = jnp.where(source >= 0, valid_ref[jnp.maximum(source, 0)], 0)
+            live = live | ((column >= o * stretch_len) & (column < o * stretch_len + length))
+        bias_ref[a] = jnp.where(seen & live, 0.0, NEG)
+        return carry
+
+    lax.fori_loop(0, stretch_len // BLOCK, see, 0)
 
     for j in range(hops):
 
@@ -219,6 +219,8 @@
     def _():
         arrive(cache_copies(0))
         hop(0, 0).start()
+
+    start(fresh_copies(0))
 
     def attend_head(h):
         blocks = rows // BLOCK
@@ -232,7 +234,7 @@
                 [k[...] for k in k_parts],
                 [v[...] for v in v_parts],
                 bias_ref[pl.ds(i * blocks, blocks)],
-                live_ref[pl.ds(at, rows)],
+                lax.broadcasted_iota(jnp.int32, (rows, 1), 0) + at < valid_ref[c],
                 fold,
             )
             return carry
@@ -299,17 +301,17 @@
                 hop(j, g).wait_send()
 
         remote, local = out_copies(g)
-        for copy in remote:
+        for copy in remote + local:
             copy.wait()
-        local.wait()
         return carry
 
     lax.fori_loop(0, groups, finish, 0)
 
 
-def exchange_and_attend(cache, fresh, bias, row_live):
+def exchange_and_attend(cache, fresh, block_list, block_count, valid_tokens):
     space = lax.axis_size("space")
-    _, all_heads, tokens, d = fresh.shape
+    all_heads, tokens, d = fresh[0].shape
+    dtype = fresh[0].dtype
     heads, stretch_len = all_heads // space, tokens * space
     groups = max(n for n in range(1, GROUPS + 1) if heads % n == 0)
     fold = math.log2(math.e) / math.sqrt(d)
@@ -317,23 +319,22 @@
     dma = pltpu.SemaphoreType.DMA
     return pl.pallas_call(
         functools.partial(exchange_kernel, fold, rows, groups),
-        out_shape=jax.ShapeDtypeStruct((all_heads, tokens, d), fresh.dtype),
-        in_specs=[
-            pl.BlockSpec(memory_space=pl.ANY),
-            pl.BlockSpec(memory_space=pl.ANY),
-            pl.BlockSpec(memory_space=pltpu.VMEM),
-            pl.BlockSpec(memory_space=pltpu.VMEM),
-        ],
+        out_shape=jax.ShapeDtypeStruct((all_heads, tokens, d), dtype),
+        in_specs=[pl.BlockSpec(memory_space=pl.ANY)] * 5
+        + [pl.BlockSpec(memory_space=pltpu.SMEM)] * 3,
         out_specs=pl.BlockSpec(memory_space=pl.ANY),
         scratch_shapes=[
-            pltpu.VMEM((2, heads, stretch_len, d), fresh.dtype),
-            pltpu.VMEM((WIN - 1, 2, heads, stretch_len, d), fresh.dtype),
-            pltpu.VMEM((3, heads, stretch_len, d), fresh.dtype),
-            pltpu.VMEM((heads, stretch_len, d), fresh.dtype),
+            pltpu.VMEM((2, heads, stretch_len, d), dtype),
+            pltpu.VMEM((WIN - 1, 2, heads, stretch_len, d), dtype),
+            pltpu.VMEM((3, heads, stretch_len, d), dtype),
+            pltpu.VMEM((heads, stretch_len, d), dtype),
+            pltpu.VMEM((stretch_len // BLOCK, 1, WIN * stretch_len), jnp.float32),
         ]
-        + [dma((groups, space - 1))] * 6
+        + [dma((2, groups, space - 1))] * 2
+        + [dma((3, groups, space - 1))] * 2
+        + [dma((groups, space - 1))] * 2
         + [dma((WIN - 1, groups))] * 2
-        + [dma((3, groups))],
+        + [dma((2, groups)), dma((3, groups)), dma((groups,))],
         compiler_params=pltpu.CompilerParams(
             collective_id=0, has_side_effects=True, vmem_limit_bytes=50 * 1024 * 1024
         ),
@@ -342,7 +343,7 @@
             bytes_accessed=12 * heads * stretch_len * d,
             transcendentals=heads * stretch_len * WIN * stretch_len,
         ),
-    )(cache, fresh, bias, row_live)
+    )(*cache, *fresh, block_list, block_count, valid_tokens)
 
 
 def on_device(
@@ -355,21 +356,15 @@
     block_count,
     valid_tokens,
 ):
-    stretch_now = lax.axis_index("tm")
-    space = lax.axis_size("space")
-    stretch_len = queries.shape[1] * space
-
-    def by_heads(*arrays):
-        return jnp.transpose(jnp.concatenate(arrays, 0), (0, 2, 1, 3))
-
-    bias, row_live = window_bias(
-        stretch_now, stretch_len, block_list[0], block_count[0], valid_tokens
-    )
+    def by_heads(x):
+        return jnp.transpose(x[0], (1, 0, 2))
+
     back = exchange_and_attend(
-        by_heads(cache_keys, cache_values),
-        by_heads(queries, noisy_keys, noisy_values),
-        bias,
-        row_live,
+        (by_heads(cache_keys), by_heads(cache_values)),
+        (by_heads(queries), by_heads(noisy_keys), by_heads(noisy_values)),
+        block_list[0],
+        block_count[0],
+        valid_tokens,
     )
     return jnp.transpose(back, (1, 0, 2))[None]
 

time: 140 us -> 132 us (0.943)
  other arithmetic: 8.04 us -> 0 us
    transpose x0 -> x2, local copies, waits for them, and re-layouts: none -> 5.25 us  [by_heads(): return jnp.transpose(x[0], (1, 0, 2))]
    transpose x2 -> x0, other arithmetic: 4.34 us -> none  [by_heads(): return jnp.transpose(jnp.concatenate(arrays, 0), (0, 2, 1, 3))]
    unnamed x14 -> x15, local copies, waits for them, and re-layouts: 5.57 us -> 2.36 us
    reduce_sum x2 -> x0, other arithmetic: 2.13 us -> none  [the longest x1 1.29 us: window_bias(): own = jnp.sum(jnp.where(stretches == stretch_now, valid_tokens, 0))]
    pallas_call x1, Pallas kernels: 123 us -> 122 us  [exchange_and_attend(): pl.pallas_call(functools.partial(exchange_kernel, fold, rows, groups), ou...]
where the time goes in v3:
time: 132 us; the launch traced here: 131 us
  Pallas kernels  122 us (92%)
  local copies, waits for them, and re-layouts  9.77 us (7%)
    pallas_call x1, Pallas kernels, exchange_and_attend(): pl.pallas_call(functools.partial(exchange_kernel, fold, rows, groups), ou...  122 us
    transpose x2, local copies, waits for them, and re-layouts, by_heads(): return jnp.transpose(x[0], (1, 0, 2))  5.25 us

profile of v3, /device:TPU:16, one launch (start us, length us, event | category | flops | bytes accessed | tf_op | source)
XLA Modules:
  0.0 131.4 jit_solution(3029014614325522873)
XLA Ops:
  0.0 0.0 copy-start.3
  0.0 0.0 copy-start.4
  0.0 2.0 %copy.20 = bf16[1,128,48,128]{3,1,2,0:T(8,128)(2,1)S(1)} copy(bf16[1,128,48,128]{3,2,1,0:T(8,128)(2,1)} %param.11) | data formatting | bytes 3145728 | tf_op args[3]
  2.0 0.0 copy-done.3
  2.0 0.4 copy-done.4
  2.4 0.0 copy-start.5
  2.4 0.0 copy-start.6
  2.4 2.6 %copy_bitcast_fusion.2 = (bf16[48,128,128]{2,1,0:T(8,128)(2,1)}, bf16[48,128,128]{2,1,0:T(8,128)(2,1)}) fusion(bf16[1,128,48,128]{3,2,1,0:T(8,128)(2,1)S(1)} %copy-done.3, bf16[1,128,48,128]{3,2,1,0:T(8,128)(2,1)S(1)} %copy-done.4), kind=kLoop, calls=%fused_computation.2 | loop fusion | bytes 6291456 | tf_op jit(solution)/shard_map/transpose | solution.py:360
  5.0 0.0 copy-done.5
  5.0 0.0 copy-done.6
  5.0 0.0 copy-start
  5.0 0.0 copy-start.1
  5.0 0.0 copy-start.2
  5.0 2.6 %copy_bitcast_fusion = (bf16[48,128,128]{2,1,0:T(8,128)(2,1)}, bf16[48,128,128]{2,1,0:T(8,128)(2,1)}) fusion(bf16[1,128,48,128]{3,2,1,0:T(8,128)(2,1)S(1)} %copy-done.5, bf16[1,128,48,128]{3,2,1,0:T(8,128)(2,1)S(1)} %copy-done.6), kind=kLoop, calls=%fused_computation | loop fusion | bytes 6291456 | tf_op jit(solution)/shard_map/transpose | solution.py:360
  7.6 0.0 copy-done
  7.6 0.0 copy-done.1
  7.6 0.0 copy-done.2
  7.6 121.6 %shard_map.82 = bf16[48,128,128]{2,1,0:T(8,128)(2,1)S(1)} custom-call(bf16[48,128,128]{2,1,0:T(8,128)(2,1)S(1)} %bitcast.26, bf16[48,128,128]{2,1,0:T(8,128)(2,1)} %get-tuple-element.8.cv_in, bf16[48,128,128]{2,1,0:T(8,128)(2,1)} %get-tuple-element.7.q_in, bf16[48,128,128]{2,1,0:T(8,128)(2,1)} %get-tuple-element.6.k_in, ...), custom_call_target="tpu_custom_call" | custom-call | flops 6442450944 | bytes 9437184 | tf_op jit(solution)/shard_map/pallas_call | solution.py:320
  129.2 2.2 %copy.14 = bf16[1,128,48,128]{3,2,1,0:T(8,128)(2,1)} copy(bf16[1,128,48,128]{3,1,2,0:T(8,128)(2,1)S(1)} %bitcast.27) | data formatting | bytes 3145728 | tf_op jit(solution)/shard_map/broadcast_in_dim | solution.py:369
Async XLA Ops:
  0.0 2.0 %copy-start.3 = (bf16[1,128,48,128]{3,2,1,0:T(8,128)(2,1)S(1)}, bf16[1,128,48,128]{3,2,1,0:T(8,128)(2,1)}, u32[]{:S(2)}) copy-start(bf16[1,128,48,128]{3,2,1,0:T(8,128)(2,1)} %param.8) | copy-start | bytes 4718596
  0.0 2.4 %copy-start.4 = (bf16[1,128,48,128]{3,2,1,0:T(8,128)(2,1)S(1)}, bf16[1,128,48,128]{3,2,1,0:T(8,128)(2,1)}, u32[]{:S(2)}) copy-start(bf16[1,128,48,128]{3,2,1,0:T(8,128)(2,1)} %param.12) | copy-start | bytes 4718596
  2.4 2.6 %copy-start.5 = (bf16[1,128,48,128]{3,2,1,0:T(8,128)(2,1)S(1)}, bf16[1,128,48,128]{3,2,1,0:T(8,128)(2,1)}, u32[]{:S(2)}) copy-start(bf16[1,128,48,128]{3,2,1,0:T(8,128)(2,1)} %param.10) | copy-start | bytes 4718596
  2.4 2.6 %copy-start.6 = (bf16[1,128,48,128]{3,2,1,0:T(8,128)(2,1)S(1)}, bf16[1,128,48,128]{3,2,1,0:T(8,128)(2,1)}, u32[]{:S(2)}) copy-start(bf16[1,128,48,128]{3,2,1,0:T(8,128)(2,1)} %param.9) | copy-start | bytes 4718596
  5.0 2.6 %copy-start = (s32[1,4,12]{2,1,0:T(4,128)S(1)}, s32[1,4,12]{2,1,0:T(4,128)}, u32[]{:S(2)}) copy-start(s32[1,4,12]{2,1,0:T(4,128)} %param.13) | copy-start | bytes 580
  5.0 2.6 %copy-start.1 = (s32[1,4]{1,0:T(1,128)S(1)}, s32[1,4]{1,0:T(1,128)}, u32[]{:S(2)}) copy-start(s32[1,4]{1,0:T(1,128)} %param.14) | copy-start | bytes 52
  5.0 2.6 %copy-start.2 = (s32[8]{0:T(128)S(1)}, s32[8]{0:T(128)}, u32[]{:S(2)}) copy-start(s32[8]{0:T(128)} %valid_ref.1) | copy-start | bytes 100
